TPU v7x, 256 devices: a whole 4x4x8 slice. The times are simulated.
256 devices in a mesh: ctx: 32 (over z, y_lo, core), head: 8 (over x, y_hi).
Axes of the slice: x: 4, y: 4 (y_hi: 2, y_lo: 2; y = y_hi * 2 + y_lo), z: 8, core: 2. Of those that a mesh axis runs over, the one named last changes fastest.
Arguments:
- queries: bfloat16 [16384, 4096], P('ctx', 'head'), may hold values from -180 to 180
- keys_values: bfloat16 [2, 16384, 1024], P(None, 'ctx', 'head'), may hold values from -6 to 6
- trace_lengths: int32 [7], replicated, may hold values from 1 to 4096, as said below
- step_rows: int32 [7, 32], replicated, may hold values from 0 to 16383, as said below
- prompt_ids: int32 [7], replicated, may hold values from 0 to 1
- cluster_ids: int32 [7], replicated, may hold values from 0 to 3
- step_stream: bfloat16 [224, 8192], P(None, 'ctx'), may hold values from -0.29882812 to 0.29882812
- out_weight: bfloat16 [4096, 8192], P('head', 'ctx'), may hold values from -3.59375 to 3.59375
- score_weight: bfloat16 [8192, 8192], P('ctx', 'head'), may hold values from -0.0625 to 0.0625
- class_weight: bfloat16 [8192, 2], P('head'), may hold values from -0.125 to 0.125
Outputs:
- attended: float32 [16384, 4096], P('ctx', 'head')
- step_scores: float32 [7, 32], replicated
- votes: float32 [2, 4], replicated
Inputs may be any that keep to these rules, and one draw needn't show every extreme that they name: `trace_lengths`: the traces lie end to end from row 0 and fill the context; one trace has exactly 4096 rows. `step_rows`: each trace's step rows lie inside that trace and rise strictly; the last one is the trace's last row.
All inputs are finite; a program needn't handle non-finite values.
Results may differ from a plain program's by a relative error of at most 0.033.
Values may be sent and summed in bfloat16 or wider, within the bound.
No kernel may reach another device: no remote copies, remote signals or barrier semaphores. Data moves between devices by JAX's collectives and lax.ppermute only.
A program may use at most 64 MiB of HBM per device.

v0:
```python
import jax
import jax.numpy as jnp
from jax import lax
from jax.sharding import PartitionSpec as P

HD = 128
PROMPTS = 2
CLUSTERS = 4


def passed_along(value, axis, steps):
    count = lax.axis_size(axis)
    initial, last = (max(0, -steps), min(count, count - steps))
    return lax.ppermute(value, axis, [(source, source + steps) for source in range(initial, last)])


def trace_of(positions, trace_ends):
    return jnp.sum((positions[:, None] >= trace_ends[None, :]).astype(jnp.int32), axis=1)


def per_device(
    queries,
    keys_values,
    trace_lengths,
    step_rows,
    prompt_ids,
    cluster_ids,
    step_stream,
    out_weight,
    score_weight,
    class_weight,
):
    tok_rows = queries.shape[0]
    ctx_count = lax.axis_size("ctx")
    all_rows = tok_rows * ctx_count
    longest = all_rows // 4
    reach_steps = (longest + tok_rows - 2) // tok_rows
    kv_heads = keys_values.shape[2] // HD
    q_heads = queries.shape[1] // HD
    per_group = q_heads // kv_heads
    my_block = lax.axis_index("ctx")
    trace_ends = jnp.cumsum(trace_lengths)
    local_pos = my_block * tok_rows + jnp.arange(tok_rows, dtype=jnp.int32)
    q_owner = trace_of(local_pos, trace_ends)
    q_blocks = queries.reshape(tok_rows, kv_heads, per_group, HD)
    score_scale = HD ** (-0.5)

    def attend(state_now, kv_block, source):
        key_pos = source * tok_rows + jnp.arange(tok_rows, dtype=jnp.int32)
        k_owner = trace_of(key_pos, trace_ends)
        allowed = (q_owner[:, None] == k_owner[None, :]) & (key_pos[None, :] <= local_pos[:, None])
        allowed = allowed & (key_pos[None, :] >= 0)

        def compute(state_in):
            running_max, weight_sum, summed = state_in
            keys_blk = kv_block[0].reshape(tok_rows, kv_heads, HD)
            values_blk = kv_block[1].reshape(tok_rows, kv_heads, HD)
            logits_blk = (
                jnp.einsum("qhgd,khd->hgqk", q_blocks, keys_blk, preferred_element_type=jnp.float32)
                * score_scale
            )
            logits_blk = jnp.where(allowed[None, None], logits_blk, -jnp.inf)
            new_max = jnp.maximum(running_max, jnp.max(logits_blk, axis=3))
            rescale = jnp.exp(running_max - new_max)
            weights = jnp.exp(logits_blk - new_max[..., None])
            weight_sum = weight_sum * rescale + jnp.sum(weights, axis=3)
            product = jnp.einsum(
                "hgqk,khd->qhgd",
                weights.astype(jnp.bfloat16),
                values_blk,
                preferred_element_type=jnp.float32,
            )
            summed = summed * jnp.transpose(rescale, (2, 0, 1))[..., None] + product
            return (new_max, weight_sum, summed)

        return lax.cond(jnp.any(allowed), compute, lambda state_in: state_in, state_now)

    start_state = (
        jnp.full((kv_heads, per_group, tok_rows), -jnp.inf, jnp.float32),
        jnp.zeros((kv_heads, per_group, tok_rows), jnp.float32),
        jnp.zeros((tok_rows, kv_heads, per_group, HD), jnp.float32),
    )
    state_now = attend(start_state, keys_values, my_block)
    moving = keys_values
    for offset in range(1, reach_steps + 1):
        moving = passed_along(moving, "ctx", 1)
        state_now = attend(state_now, moving, my_block - offset)
    running_max, weight_sum, summed = state_now
    normed = summed / jnp.transpose(weight_sum, (2, 0, 1))[..., None]
    attended = normed.reshape(tok_rows, q_heads * HD)
    flat_rows = step_rows.reshape(-1)
    selector = (flat_rows[:, None] == local_pos[None, :]).astype(jnp.float32)
    chosen = jnp.dot(
        selector, attended, precision=lax.Precision.HIGHEST, preferred_element_type=jnp.float32
    )
    picked = lax.psum(chosen.astype(jnp.bfloat16), "ctx")
    partial_proj = jnp.dot(picked, out_weight, preferred_element_type=jnp.float32)
    projected = lax.psum(partial_proj, "head")
    stream = (step_stream.astype(jnp.float32) + projected).astype(jnp.bfloat16)
    inner = lax.psum(jnp.dot(stream, score_weight, preferred_element_type=jnp.float32), "ctx")
    hidden = jnp.maximum(inner, 0.0).astype(jnp.bfloat16)
    partial_logits = jnp.dot(hidden, class_weight, preferred_element_type=jnp.float32)
    logits = lax.psum(partial_logits, "head")
    step_scores = jax.nn.sigmoid(logits[:, 1] - logits[:, 0]).reshape(step_rows.shape)
    chain = jnp.min(step_scores, axis=1)
    prompt_mask = (prompt_ids[:, None] == jnp.arange(PROMPTS, dtype=jnp.int32)[None, :]).astype(
        jnp.float32
    )
    cluster_mask = (cluster_ids[:, None] == jnp.arange(CLUSTERS, dtype=jnp.int32)[None, :]).astype(
        jnp.float32
    )
    votes = jnp.sum(
        prompt_mask[:, :, None] * cluster_mask[:, None, :] * chain[:, None, None], axis=0
    )
    return (attended, step_scores, votes)


def solution(mesh):
    placed = (
        P("ctx", "head"),
        P(None, "ctx", "head"),
        P(),
        P(),
        P(),
        P(),
        P(None, "ctx"),
        P("head", "ctx"),
        P("ctx", "head"),
        P("head", None),
    )
    return jax.shard_map(
        per_device,
        mesh=mesh,
        in_specs=placed,
        out_specs=(P("ctx", "head"), P(), P()),
        check_vma=False,
    )
```

profile of v0, /device:TPU:1, one launch (start us, length us, event | category | flops | bytes accessed | tf_op | source)
XLA Modules:
  0.0 584.1 jit_solution(6168985343166211971)
XLA Ops:
  7.2 4.7 collective-permute-start
  12.0 3.6 collective-permute-done
  15.6 4.3 collective-permute-start.1
  19.9 3.3 collective-permute-done.1
  23.2 4.4 collective-permute-start.2
  27.6 3.3 collective-permute-done.2
  30.8 4.4 collective-permute-start.3
  35.3 3.2 collective-permute-done.3
  38.5 4.4 collective-permute-start.4
  42.9 3.3 collective-permute-done.4
  46.2 4.4 collective-permute-start.5
  51.6 2.3 collective-permute-done.5
  53.9 4.4 collective-permute-start.6
  58.3 3.6 and_and_fusion
  67.0 5.8 %collective-permute-start.7 = (bf16[2,512,128]{2,1,0:T(8,128)(2,1)}, bf16[2,512,128]{2,1,0:T(8,128)(2,1)}, u32[]{:S(2)}, u32[]{:S(2)}) collective-permute-start(bf16[2,512,128]{2,1,0:T(8,128)(2,1)} %collective-permute-done.6), channel_id=1, source_target_pairs={{0,8},{8,16},{16,24},{24,32},{32,40},{40,48},{48,56},{56,64},{64,7... | collective-permute-start | bytes 786440 | tf_op jit(solution)/shard_map/ppermute | solution.py:14
  72.8 3.0 fusion.214
  78.5 6.9 %conditional.9 = (f32[1,4,512]{2,1,0:T(4,128)}, f32[1,4,512]{2,1,0:T(4,128)S(1)}, f32[512,1,4,128]{3,0,2,1:T(8,128)S(1)}) conditional(s32[]{:T(128)} %convert_element_type.126, () %tuple.65, (pred[512,512]{0,1:T(8,128)(4,1)}, bf16[2,512,128]{2,1,0:T(8,128)(2,1)}, bf16[512,1,4,128]{0,3,2,1:T(8,128)(2,1)S(1)}) %tuple.190), branch_computations={%region_19.20_spmd, %region_20.23_spmd} | conditional | flops 548669440 | bytes 17375312 | solution.py:76
  78.5 2.5 fusion.2
  83.3 2.0 fusion.10
  85.4 6.3 %conditional.10 = ((f32[1,4,512]{2,1,0:T(4,128)}, f32[1,4,512]{2,1,0:T(4,128)S(1)}, f32[512,1,4,128]{3,0,2,1:T(8,128)S(1)})) conditional(s32[]{:T(128)} %convert_element_type.125, (f32[1,4,512]{2,1,0:T(4,128)}, f32[1,4,512]{2,1,0:T(4,128)S(1)}, f32[512,1,4,128]{3,0,2,1:T(8,128)S(1)}) %conditional.9, (pred[512,512]{0,1:T(8,128)(4,1)S(1)}, ...), branch_computations={%region_23.24_spmd, %region_24.0_spmd} | conditional | flops 548935680 | bytes 17432636 | solution.py:76
  100.1 253.1 %all-reduce.4.cloned.1.call-done = bf16[224,512]{1,0:T(8,128)(2,1)} async-done(((bf16[224,512]{1,0:T(8,128)(2,1)}), bf16[224,512]{1,0:T(8,128)(2,1)}) %all-reduce.4.cloned.1.call-update) | async-done | bytes 229392 | tf_op jit(solution)/shard_map/psum | solution.py:96
  355.1 86.1 %all-reduce.6.cloned.1.call-done = f32[224,256]{1,0:T(8,128)} async-done(((f32[224,256]{1,0:T(8,128)}), f32[224,256]{1,0:T(8,128)}) %all-reduce.6.cloned.1.call-update) | async-done | bytes 229392 | tf_op jit(solution)/shard_map/psum | solution.py:98
  442.4 115.0 %all-reduce.7 = bf16[224,1024]{1,0:T(8,128)(2,1)S(1)} all-reduce(f32[224,1024]{1,0:T(8,128)S(1)} %fusion.204), channel_id=1, replica_groups=mesh['ctx'=32,'head'=8] {'ctx'}, use_global_device_ids=true, to_apply=%region_57.58 | all-reduce | flops 229376 | bytes 1376256 | tf_op jit(solution)/shard_map/psum | solution.py:100
  557.6 18.7 %psum.31 = f32[224,2]{0,1:T(2,128)S(1)} all-reduce(f32[224,2]{0,1:T(2,128)S(1)} %fusion.199), channel_id=1, replica_groups=mesh['ctx'=32,'head'=8] {'head'}, use_global_device_ids=true, to_apply=%region_58.59 | all-reduce | flops 448 | bytes 3584 | tf_op jit(solution)/shard_map/psum | solution.py:103
  (96 shorter events, 24.2 us)
Async XLA Ops:
  7.2 434.0 %copy-start = (bf16[256,1024]{1,0:T(8,128)(2,1)S(1)}, bf16[256,1024]{1,0:T(8,128)(2,1)}, u32[]{:S(2)}) copy-start(bf16[256,1024]{1,0:T(8,128)(2,1)} %param.36) | copy-start | bytes 1572868
  7.2 346.0 %all-reduce.4.cloned.1.call-start = ((), (), s32[]{:S(2)}) async-start(), calls=%async_computation | async-start | bytes 458752 | tf_op jit(solution)/shard_map/psum | solution.py:96
  7.2 8.3 %collective-permute-start = (bf16[2,512,128]{2,1,0:T(8,128)(2,1)}, bf16[2,512,128]{2,1,0:T(8,128)(2,1)S(1)}, u32[]{:S(2)}, u32[]{:S(2)}) collective-permute-start(bf16[2,512,128]{2,1,0:T(8,128)(2,1)} %param.29), channel_id=1, source_target_pairs={{0,8},{8,16},{16,24},{24,32},{32,40},{40,48},{48,56},{56,64},{64,7... | collective-permute-start | bytes 786440 | tf_op jit(solution)/shard_map/ppermute | solution.py:14
  15.6 7.6 %copy-start.19 = (bf16[2,512,128]{2,1,0:T(8,128)(2,1)}, bf16[2,512,128]{2,1,0:T(8,128)(2,1)S(1)}, u32[]{:S(2)}) copy-start(bf16[2,512,128]{2,1,0:T(8,128)(2,1)S(1)} %collective-permute-done) | copy-start | bytes 786436
  15.6 7.6 %collective-permute-start.1 = (bf16[2,512,128]{2,1,0:T(8,128)(2,1)S(1)}, bf16[2,512,128]{2,1,0:T(8,128)(2,1)S(1)}, u32[]{:S(2)}, u32[]{:S(2)}) collective-permute-start(bf16[2,512,128]{2,1,0:T(8,128)(2,1)S(1)} %collective-permute-done), channel_id=1, source_target_pairs={{0,8},{8,16},{16,24},{24,32},{32,40},{40,48},{48,56},{56,64},{64,7... | collective-permute-start | bytes 786440 | tf_op jit(solution)/shard_map/ppermute | solution.py:14
  23.2 4.4 copy-start.17
  23.2 7.7 %collective-permute-start.2 = (bf16[2,512,128]{2,1,0:T(8,128)(2,1)S(1)}, bf16[2,512,128]{2,1,0:T(8,128)(2,1)S(1)}, u32[]{:S(2)}, u32[]{:S(2)}) collective-permute-start(bf16[2,512,128]{2,1,0:T(8,128)(2,1)S(1)} %collective-permute-done.1), channel_id=1, source_target_pairs={{0,8},{8,16},{16,24},{24,32},{32,40},{40,48},{48,56},{56,64},{64,7... | collective-permute-start | bytes 786440 | tf_op jit(solution)/shard_map/ppermute | solution.py:14
  30.8 4.4 copy-start.15
  30.8 7.7 %collective-permute-start.3 = (bf16[2,512,128]{2,1,0:T(8,128)(2,1)S(1)}, bf16[2,512,128]{2,1,0:T(8,128)(2,1)S(1)}, u32[]{:S(2)}, u32[]{:S(2)}) collective-permute-start(bf16[2,512,128]{2,1,0:T(8,128)(2,1)S(1)} %collective-permute-done.2), channel_id=1, source_target_pairs={{0,8},{8,16},{16,24},{24,32},{32,40},{40,48},{48,56},{56,64},{64,7... | collective-permute-start | bytes 786440 | tf_op jit(solution)/shard_map/ppermute | solution.py:14
  38.5 23.4 %copy-start.13 = (bf16[2,512,128]{2,1,0:T(8,128)(2,1)}, bf16[2,512,128]{2,1,0:T(8,128)(2,1)S(1)}, u32[]{:S(2)}) copy-start(bf16[2,512,128]{2,1,0:T(8,128)(2,1)S(1)} %collective-permute-done.3) | copy-start | bytes 786436
  38.5 7.7 %collective-permute-start.4 = (bf16[2,512,128]{2,1,0:T(8,128)(2,1)S(1)}, bf16[2,512,128]{2,1,0:T(8,128)(2,1)S(1)}, u32[]{:S(2)}, u32[]{:S(2)}) collective-permute-start(bf16[2,512,128]{2,1,0:T(8,128)(2,1)S(1)} %collective-permute-done.3), channel_id=1, source_target_pairs={{0,8},{8,16},{16,24},{24,32},{32,40},{40,48},{48,56},{56,64},{64,7... | collective-permute-start | bytes 786440 | tf_op jit(solution)/shard_map/ppermute | solution.py:14
  46.2 15.7 %copy-start.11 = (bf16[2,512,128]{2,1,0:T(8,128)(2,1)}, bf16[2,512,128]{2,1,0:T(8,128)(2,1)S(1)}, u32[]{:S(2)}) copy-start(bf16[2,512,128]{2,1,0:T(8,128)(2,1)S(1)} %collective-permute-done.4) | copy-start | bytes 786436
  46.2 7.7 %collective-permute-start.5 = (bf16[2,512,128]{2,1,0:T(8,128)(2,1)S(1)}, bf16[2,512,128]{2,1,0:T(8,128)(2,1)S(1)}, u32[]{:S(2)}, u32[]{:S(2)}) collective-permute-start(bf16[2,512,128]{2,1,0:T(8,128)(2,1)S(1)} %collective-permute-done.4), channel_id=1, source_target_pairs={{0,8},{8,16},{16,24},{24,32},{32,40},{40,48},{48,56},{56,64},{64,7... | collective-permute-start | bytes 786440 | tf_op jit(solution)/shard_map/ppermute | solution.py:14
  53.9 24.6 %copy-start.9 = (bf16[2,512,128]{2,1,0:T(8,128)(2,1)}, bf16[2,512,128]{2,1,0:T(8,128)(2,1)S(1)}, u32[]{:S(2)}) copy-start(bf16[2,512,128]{2,1,0:T(8,128)(2,1)S(1)} %collective-permute-done.5) | copy-start | bytes 786436
  53.9 13.1 %collective-permute-start.6 = (bf16[2,512,128]{2,1,0:T(8,128)(2,1)S(1)}, bf16[2,512,128]{2,1,0:T(8,128)(2,1)}, u32[]{:S(2)}, u32[]{:S(2)}) collective-permute-start(bf16[2,512,128]{2,1,0:T(8,128)(2,1)S(1)} %collective-permute-done.5), channel_id=1, source_target_pairs={{0,8},{8,16},{16,24},{24,32},{32,40},{40,48},{48,56},{56,64},{64,7... | collective-permute-start | bytes 786440 | tf_op jit(solution)/shard_map/ppermute | solution.py:14
  67.0 29.6 %collective-permute-start.7 = (bf16[2,512,128]{2,1,0:T(8,128)(2,1)}, bf16[2,512,128]{2,1,0:T(8,128)(2,1)}, u32[]{:S(2)}, u32[]{:S(2)}) collective-permute-start(bf16[2,512,128]{2,1,0:T(8,128)(2,1)} %collective-permute-done.6), channel_id=1, source_target_pairs={{0,8},{8,16},{16,24},{24,32},{32,40},{40,48},{48,56},{56,64},{64,7... | collective-permute-start | bytes 786440 | tf_op jit(solution)/shard_map/ppermute | solution.py:14
  78.5 4.8 copy-start.8
  97.5 255.7 %copy-start.6 = (bf16[512,256]{1,0:T(8,128)(2,1)S(1)}, bf16[512,256]{1,0:T(8,128)(2,1)}, u32[]{:S(2)}) copy-start(bf16[512,256]{1,0:T(8,128)(2,1)} %param.35) | copy-start | bytes 786436
  97.5 257.6 %copy-start.24 = (s32[7]{0:T(128)S(1)}, s32[7]{0:T(128)}, u32[]{:S(2)}) copy-start(s32[7]{0:T(128)} %param.32) | copy-start | bytes 88
  97.5 257.6 %copy-start.22 = (s32[7]{0:T(128)S(1)}, s32[7]{0:T(128)}, u32[]{:S(2)}) copy-start(s32[7]{0:T(128)} %param.33) | copy-start | bytes 88
  97.5 343.7 %copy-start.7 = (bf16[224,256]{1,0:T(8,128)(2,1)S(1)}, bf16[224,256]{1,0:T(8,128)(2,1)}, u32[]{:S(2)}) copy-start(bf16[224,256]{1,0:T(8,128)(2,1)} %param.34) | copy-start | bytes 344068
  98.5 458.8 %copy-start.23 = (bf16[1024,2]{0,1:T(2,128)(2,1)S(1)}, bf16[1024,2]{0,1:T(2,128)(2,1)}, u32[]{:S(2)}) copy-start(bf16[1024,2]{0,1:T(2,128)(2,1)} %param.37) | copy-start | bytes 12292
  98.6 478.6 %copy-start.1 = (f32[64,8,4,128]{3,1,2,0:T(8,128)}, f32[64,8,4,128]{3,1,2,0:T(8,128)S(1)}, u32[]{:S(2)}) copy-start(f32[64,8,4,128]{3,1,2,0:T(8,128)S(1)} %copy.74) | copy-start | bytes 3145732
  100.0 341.1 %all-reduce.6.cloned.1.call-start = ((), (), s32[]{:S(2)}) async-start(), calls=%async_computation.1 | async-start | bytes 458752 | tf_op jit(solution)/shard_map/psum | solution.py:98
  (10 other events, 12.6 us)
Sparse Core Ops, SparseCore 0:
  100.1 252.9 all-reduce.3
  356.0 85.1 all-reduce.5
where the time goes:
time: 591 us; the launch traced here: 584 us
  waiting for transfers between devices  358 us (61%)
  blocking collectives  134 us (23%)
  starting transfers between devices  36.8 us (6%)
  between operations  20.1 us (3%)
  other arithmetic  13.4 us (2%)
  matrix products  12.5 us (2%)
  local copies, waits for them, and re-layouts  9.28 us (2%)
    psum x1, waiting for transfers between devices, per_device(): picked = lax.psum(chosen.astype(jnp.bfloat16), 'ctx')  253 us
    psum x1, blocking collectives, per_device(): lax.psum(jnp.dot(stream, score_weight, preferred_element_type=jnp.float32...  115 us
    psum x1, waiting for transfers between devices, per_device(): projected = lax.psum(partial_proj, 'head')  86.1 us
    ppermute x8, starting transfers between devices, passed_along(): lax.ppermute(value, axis, [(source, source + steps) for source in range(i...  36.7 us
    ppermute x8, waiting for transfers between devices, passed_along(): lax.ppermute(value, axis, [(source, source + steps) for source in range(i...  19 us
    psum x1, blocking collectives, per_device(): logits = lax.psum(partial_logits, 'head')  18.7 us
  transfers between devices with their start and end apart: 10, of which 8 were waited for; matrix products, arithmetic and copies ran while one was open for 4% of the time, Pallas kernels for 0%

commit v1 on v0

v1 whole, which is shorter than its diff:
```python
import functools
import math

import jax
import jax.numpy as jnp
from jax import lax
from jax.experimental import pallas as pl
from jax.experimental.pallas import tpu as pltpu
from jax.sharding import PartitionSpec as P

HD = 128
PROMPTS = 2
CLUSTERS = 4
TRACES = 7
STEPS = 32
PER_GROUP = 4
BLOCK = 512
TILE = 256
Z = 8
PLANE = 4
PAD = 8
GROUP = Z * PAD
WIDE = 1024
COEF = HD**-0.5 * math.log2(math.e)
LOW = -1e30
VMEM = pl.BlockSpec(memory_space=pltpu.VMEM)
SMEM = pl.BlockSpec(memory_space=pltpu.SMEM)
BF16 = jnp.bfloat16
F32 = jnp.float32


def first_key(row, lengths):
    start = row * 0
    end = jnp.int32(0)
    for t in range(TRACES):
        end = end + lengths[t]
        start = jnp.where(row >= end, end, start)
    return start


def attend_kernel(slots, first, last, *refs):
    refs = list(refs)
    me_ref, lengths, q_ref = refs[:3]
    kv_refs = refs[3 : 3 + len(slots)]
    refs = refs[3 + len(slots) :]
    if last:
        rows_ref, refs = refs[0], refs[1:]
    if not first:
        m_in, l_in, acc_in = refs[:3]
        refs = refs[3:]
    if last:
        out_ref, keep_ref, pass_ref, send_ref, m_ref, l_ref, acc_ref, half_ref = refs
        m_ref[...] = m_in[...]
        l_ref[...] = l_in[...]
        acc_ref[...] = acc_in[...]
    else:
        m_ref, l_ref, acc_ref = refs
        if not first:
            m_ref[...] = m_in[...]
            l_ref[...] = l_in[...]
            acc_ref[...] = acc_in[...]
    me = me_ref[0]
    place = me % PLANE
    row0 = me * BLOCK
    ones = jnp.ones((BLOCK, HD), BF16)

    def weigh(rows, h, keys, ext, mask, fresh):
        cols = slice(h * HD, (h + 1) * HD)
        s = lax.dot_general(
            q_ref[rows, cols], keys, (((1,), (1,)), ((), ())), preferred_element_type=F32
        )
        if mask is not None:
            s = jnp.where(mask, s, LOW)
        top = jnp.max(s, axis=1, keepdims=True)
        if fresh:
            top = jnp.broadcast_to(top, (TILE, HD))
        else:
            before = m_ref[rows, cols]
            top = jnp.maximum(before, top)
        wide = jnp.concatenate([top] * (s.shape[1] // HD), axis=1)
        p = jnp.exp2((s - wide) * COEF).astype(BF16)
        pv = jnp.dot(p, ext, preferred_element_type=F32)
        m_ref[rows, cols] = top
        if fresh:
            acc_ref[rows, cols] = pv[:, :HD]
            l_ref[rows, cols] = pv[:, HD:]
        else:
            scale = jnp.exp2((before - top) * COEF)
            acc_ref[rows, cols] = acc_ref[rows, cols] * scale + pv[:, :HD]
            l_ref[rows, cols] = l_ref[rows, cols] * scale + pv[:, HD:]

    def own_block(kv):
        for tile in range(BLOCK // TILE):
            width = (tile + 1) * TILE
            rows = slice(tile * TILE, width)
            keys = kv[0, :width, :]
            ext = jnp.concatenate([kv[1, :width, :], ones[:width]], axis=1)
            q_pos = row0 + tile * TILE + lax.broadcasted_iota(jnp.int32, (TILE, width), 0)
            k_pos = row0 + lax.broadcasted_iota(jnp.int32, (TILE, width), 1)
            starts = first_key(
                row0 + tile * TILE + lax.broadcasted_iota(jnp.int32, (TILE, HD), 0), lengths
            )
            starts = jnp.concatenate([starts] * (width // HD), axis=1)
            mask = (k_pos <= q_pos) & (k_pos >= starts)
            for h in range(PER_GROUP):
                weigh(rows, h, keys, ext, mask, True)

    def other_block(kv, block):
        key0 = block * BLOCK

        def one_tile(tile, carry):
            begin = pl.multiple_of(tile * TILE, TILE)
            rows = pl.ds(begin, TILE)
            low = first_key(row0 + begin, lengths)
            high = first_key(row0 + begin + TILE - 1, lengths)
            some = (block < me) & (key0 + BLOCK > low)
            every = key0 >= high

            def run(masked):
                keys = kv[0]
                ext = jnp.concatenate([kv[1], ones], axis=1)
                mask = None
                if masked:
                    starts = first_key(
                        row0 + begin + lax.broadcasted_iota(jnp.int32, (TILE, HD), 0), lengths
                    )
                    starts = jnp.concatenate([starts] * (BLOCK // HD), axis=1)
                    k_pos = key0 + lax.broadcasted_iota(jnp.int32, (TILE, BLOCK), 1)
                    mask = k_pos >= starts
                for h in range(PER_GROUP):
                    weigh(rows, h, keys, ext, mask, False)

            pl.when(some & every)(functools.partial(run, False))
            pl.when(some & jnp.logical_not(every))(functools.partial(run, True))
            return carry

        lax.fori_loop(0, BLOCK // TILE, one_tile, 0)

    for (back, flip), kv in zip(slots, kv_refs):
        if back == 0 and flip == 0:
            own_block(kv)
        else:
            other_block(kv, me - place - back * PLANE + (place ^ flip))

    if last:
        normed = acc_ref[...] / l_ref[...]
        out_ref[...] = normed
        half_ref[...] = normed.astype(BF16)
        at = lax.broadcasted_iota(jnp.int32, (PLANE * GROUP, BLOCK), 1) + row0
        chosen = jnp.where(rows_ref[...] == at, 1.0, 0.0).astype(BF16)
        got = jnp.dot(chosen, half_ref[...], preferred_element_type=F32).astype(BF16)
        keep_ref[...] = got[:GROUP]
        pass_ref[...] = got[GROUP : 2 * GROUP]
        send_ref[...] = got[2 * GROUP :]


def attend(slots, me, lengths, queries, kvs, state, rows):
    first, last = state is None, rows is not None
    heads = jax.ShapeDtypeStruct((BLOCK, PER_GROUP * HD), F32)
    operands = [me, lengths, queries, *kvs]
    specs = [SMEM, SMEM] + [VMEM] * (1 + len(kvs))
    if last:
        operands.append(rows)
        specs.append(VMEM)
    aliases = {}
    if not first:
        if not last:
            aliases = {len(operands) + k: k for k in range(3)}
        operands += state
        specs += [VMEM] * 3
    scratch = []
    if last:
        shapes = (
            heads,
            jax.ShapeDtypeStruct((GROUP, PER_GROUP * HD), BF16),
            jax.ShapeDtypeStruct((GROUP, PER_GROUP * HD), BF16),
            jax.ShapeDtypeStruct((2 * GROUP, PER_GROUP * HD), BF16),
        )
        scratch = [pltpu.VMEM((BLOCK, PER_GROUP * HD), F32)] * 3
        scratch.append(pltpu.VMEM((BLOCK, PER_GROUP * HD), BF16))
    else:
        shapes = (heads,) * 3
    work = PER_GROUP * BLOCK * BLOCK * len(slots)
    return pl.pallas_call(
        functools.partial(attend_kernel, slots, first, last),
        out_shape=shapes,
        in_specs=specs,
        out_specs=[VMEM] * len(shapes),
        scratch_shapes=scratch,
        input_output_aliases=aliases,
        compiler_params=pltpu.CompilerParams(vmem_limit_bytes=32 << 20),
        cost_estimate=pl.CostEstimate(
            flops=4 * HD * work, bytes_accessed=4 << 20, transcendentals=work
        ),
        name="attend_%d" % len(slots),
    )(*operands)


def small_call(kernel, shape, operands, specs=None, **kw):
    return pl.pallas_call(
        kernel,
        out_shape=shape,
        in_specs=specs or [VMEM] * len(operands),
        out_specs=jax.tree.map(lambda _: VMEM, shape),
        compiler_params=pltpu.CompilerParams(vmem_limit_bytes=24 << 20),
        **kw,
    )(*operands)


def project_kernel(got_ref, *refs):
    packs, out_ref = refs[:-1], refs[-1]
    got = got_ref[0].astype(F32)
    for k in range(1, Z):
        got = got + got_ref[k].astype(F32)
    got = got.astype(BF16)
    for k, pack in enumerate(packs):
        part = jnp.dot(got, pack[:BLOCK, :], preferred_element_type=F32)
        out_ref[:, k * 256 : (k + 1) * 256] = part.astype(BF16)


def inner_kernel(me_ref, mine_ref, other_ref, *refs):
    packs, out_ref = refs[:-1], refs[-1]
    place = me_ref[0] % PLANE
    at = pl.multiple_of(BLOCK + 4 * 256 + place * GROUP, GROUP)
    streams = []
    for k, pack in enumerate(packs):
        cols = slice(k * 256, (k + 1) * 256)
        total = mine_ref[:, cols].astype(F32) + other_ref[:, cols].astype(F32)
        streams.append((pack[pl.ds(at, GROUP), :].astype(F32) + total).astype(BF16))
    for n in range(4):
        inner = jnp.zeros((GROUP, 256), F32)
        for stream, pack in zip(streams, packs):
            weight = pack[BLOCK + n * 256 : BLOCK + (n + 1) * 256, :]
            inner = inner + jnp.dot(stream, weight, preferred_element_type=F32)
        out_ref[:, n * 256 : (n + 1) * 256] = inner.astype(BF16)


def hidden_kernel(me_ref, got_ref, class_ref, out_ref):
    inner = got_ref[0].astype(F32)
    for k in range(1, Z):
        inner = inner + got_ref[k].astype(F32)
    hidden = jnp.maximum(inner, 0.0).astype(BF16)
    logits = jnp.dot(hidden, class_ref[...], preferred_element_type=F32)
    gap = logits[:, 1:2] - logits[:, 0:1]
    lane = lax.broadcasted_iota(jnp.int32, (PAD, HD), 1)
    mine = jnp.where(lane == me_ref[0], gap, 0.0)
    for k in range(out_ref.shape[0]):
        out_ref[k] = mine


def vote_kernel(prompts, clusters, got_ref, scores_ref, votes_ref):
    gap = jnp.sum(got_ref[...], axis=0)
    scores = 1.0 / (1.0 + jnp.exp(-gap))
    scores_ref[...] = scores[:TRACES, :STEPS]
    lane = lax.broadcasted_iota(jnp.int32, (PAD, HD), 1)
    chain = jnp.min(jnp.where(lane < STEPS, scores, 2.0), axis=1, keepdims=True)
    prompt = lax.broadcasted_iota(jnp.int32, (PROMPTS, CLUSTERS), 0)
    cluster = lax.broadcasted_iota(jnp.int32, (PROMPTS, CLUSTERS), 1)
    votes = jnp.zeros((PROMPTS, CLUSTERS), F32)
    for t in range(TRACES):
        here = (prompt == prompts[t]) & (cluster == clusters[t])
        votes = votes + jnp.where(here, chain[t : t + 1, :], 0.0)
    votes_ref[...] = votes


def swapped(value, axis, bit):
    count = lax.axis_size(axis)
    return lax.ppermute(value, axis, [(s, s ^ bit) for s in range(count)])


def raised(value):
    count = lax.axis_size("ctx")
    return lax.ppermute(value, "ctx", [(s, (s + PLANE) % count) for s in range(count)])


def per_device(
    queries,
    keys_values,
    trace_lengths,
    step_rows,
    prompt_ids,
    cluster_ids,
    step_stream,
    out_weight,
    score_weight,
    class_weight,
):
    here = lax.axis_index("ctx").astype(jnp.int32)
    core, side = here % 2, (here // 2) % 2
    me = here.reshape(1)
    columns = [[PLANE * z + j for z in range(Z)] for j in range(PLANE)]

    kv0 = keys_values
    kv1 = raised(kv0)
    across0 = swapped(kv0, "ctx", 2)
    core0 = swapped(kv0, "ctx", 1)
    kv2 = raised(kv1)
    across1 = swapped(kv1, "ctx", 2)
    core0y = swapped(across0, "ctx", 1)
    core1 = swapped(kv1, "ctx", 1)
    across2 = swapped(kv2, "ctx", 2)
    core1y = swapped(across1, "ctx", 1)
    core2 = swapped(kv2, "ctx", 1)
    core2y = swapped(across2, "ctx", 1)

    wanted = step_rows.reshape(TRACES, Z, 2, 2).transpose(3, 2, 1, 0)
    wanted = jnp.pad(wanted, ((0, 0), (0, 0), (0, 0), (0, PAD - TRACES)), constant_values=-1)
    wanted = jnp.where(core == 1, wanted[::-1], wanted)
    wanted = jnp.where(side == 1, wanted[:, ::-1], wanted)
    wanted = wanted.reshape(PLANE * GROUP, 1)

    stream = step_stream.reshape(TRACES, Z, PLANE, 256).transpose(2, 1, 0, 3)
    stream = jnp.pad(stream, ((0, 0), (0, 0), (0, PAD - TRACES), (0, 0)))
    pack = jnp.concatenate(
        [out_weight]
        + [score_weight[:, n * 256 : (n + 1) * 256] for n in range(4)]
        + [stream.reshape(PLANE * GROUP, 256)],
        axis=0,
    )
    pack, across2 = lax.optimization_barrier((pack, across2))
    packs = [pack, swapped(pack, "ctx", 1), swapped(pack, "ctx", 2)]
    packs.append(swapped(packs[2], "ctx", 1))

    state = attend([(0, 0), (0, 1)], me, trace_lengths, queries, [kv0, core0], None, None)
    state = attend(
        [(0, 2), (0, 3), (1, 0), (1, 1)],
        me,
        trace_lengths,
        queries,
        [across0, core0y, kv1, core1],
        state,
        None,
    )
    state = attend(
        [(1, 2), (1, 3), (2, 0), (2, 1)],
        me,
        trace_lengths,
        queries,
        [across1, core1y, kv2, core2],
        state,
        None,
    )
    attended, keep, passed, sent = attend(
        [(2, 2), (2, 3)], me, trace_lengths, queries, [across2, core2y], state, wanted
    )

    arrived = swapped(sent, "ctx", 1)
    across = swapped(passed + arrived[GROUP:], "ctx", 2)
    picked = keep + arrived[:GROUP] + across
    spread = jnp.broadcast_to(picked[None], (Z, GROUP, PER_GROUP * HD))
    gathered = lax.all_to_all(spread, "ctx", 0, 0, axis_index_groups=columns)

    projected = small_call(
        project_kernel, jax.ShapeDtypeStruct((GROUP, WIDE), BF16), [gathered, *packs], name="project"
    )
    projected = projected + swapped(projected, "head", 2)
    projected = projected + swapped(projected, "head", 4)
    other = swapped(projected, "head", 1)

    inner = small_call(
        inner_kernel,
        jax.ShapeDtypeStruct((GROUP, WIDE), BF16),
        [me, projected, other, *packs],
        [SMEM] + [VMEM] * 6,
        name="inner",
    )
    inner = lax.all_to_all(
        inner.reshape(Z, PAD, WIDE), "ctx", 0, 0, axis_index_groups=columns
    )
    heads, count = lax.axis_size("head"), lax.axis_size("ctx")
    gap = small_call(
        hidden_kernel,
        jax.ShapeDtypeStruct((heads, PAD, HD), F32),
        [me, inner, class_weight],
        [SMEM, VMEM, VMEM],
        name="hidden",
    )
    gap = jnp.sum(lax.all_to_all(gap, "head", 0, 0), axis=0)
    gap = lax.all_to_all(jnp.broadcast_to(gap[None], (count, PAD, HD)), "ctx", 0, 0)
    step_scores, votes = small_call(
        vote_kernel,
        (
            jax.ShapeDtypeStruct((TRACES, STEPS), F32),
            jax.ShapeDtypeStruct((PROMPTS, CLUSTERS), F32),
        ),
        [prompt_ids, cluster_ids, gap],
        [SMEM, SMEM, VMEM],
        name="vote",
    )
    return (attended, step_scores, votes)


def solution(mesh):
    placed = (
        P("ctx", "head"),
        P(None, "ctx", "head"),
        P(),
        P(),
        P(),
        P(),
        P(None, "ctx"),
        P("head", "ctx"),
        P("ctx", "head"),
        P("head", None),
    )
    return jax.shard_map(
        per_device,
        mesh=mesh,
        in_specs=placed,
        out_specs=(P("ctx", "head"), P(), P()),
        check_vma=False,
    )
```

time: 591 us -> 152 us (0.26); the launches traced: 584 us -> 152 us
  waiting for transfers between devices: 358 us -> 64.9 us
  blocking collectives: 134 us -> 30.8 us
  between operations: 20.1 us -> 0.96 us
  Pallas kernels: 0 us -> 14.3 us
  other arithmetic: 13.4 us -> 0.13 us
  matrix products: 12.5 us -> 0 us
    psum x2 -> x0, waiting for transfers between devices: 339 us -> none  [the longest x1 253 us: per_device(): picked = lax.psum(chosen.astype(jnp.bfloat16), 'ctx')]
    psum x2 -> x0, blocking collectives: 134 us -> none  [the longest x1 115 us: per_device(): lax.psum(jnp.dot(stream, score_weight, preferred_element_type=jnp.float32...]
    all_to_all x0 -> x2, blocking collectives: none -> 30.8 us  [the longest x1 18.3 us: per_device(): lax.all_to_all(jnp.broadcast_to(gap[None], (count, PAD, HD)), 'ctx', 0, 0)]
    all_to_all x0 -> x2, waiting for transfers between devices: none -> 24.6 us  [the longest x1 17 us: per_device(): gathered = lax.all_to_all(spread, 'ctx', 0, 0, axis_index_groups=columns)]
    ppermute x8 -> x19, waiting for transfers between devices: 19 us -> 40.3 us  [the longest x17 26.9 us: swapped(): return lax.ppermute(value, axis, [(s, s ^ bit) for s in range(count)])]
    pallas_call x0 -> x8, Pallas kernels: none -> 14.3 us  [the longest x4 8.97 us: attend(): pl.pallas_call(functools.partial(attend_kernel, slots, first, last), out_...]
    dot_general x8 -> x0, matrix products: 12.5 us -> none  [the longest x2 4.32 us: compute(): jnp.einsum('qhgd,khd->hgqk', q_blocks, keys_blk, preferred_element_type=j...]
    all_to_all x0 -> x2, starting transfers between devices: none -> 12.5 us  [the longest x1 8.99 us: per_device(): gathered = lax.all_to_all(spread, 'ctx', 0, 0, axis_index_groups=columns)]
  transfers between devices with their start and end apart: 10 -> 21, of which waited for: 8 -> 9; matrix products, arithmetic and copies ran while one was open for 4% -> 2% of each run, Pallas kernels for 0% -> 6%
where the time goes in v1:
time: 152 us
  waiting for transfers between devices  64.9 us (43%)
  starting transfers between devices  36.8 us (24%)
  blocking collectives  30.8 us (20%)
  Pallas kernels  14.3 us (9%)
  local copies, waits for them, and re-layouts  4.16 us (3%)
    ppermute x17, waiting for transfers between devices, swapped(): return lax.ppermute(value, axis, [(s, s ^ bit) for s in range(count)])  26.9 us
    ppermute x17, starting transfers between devices, swapped(): return lax.ppermute(value, axis, [(s, s ^ bit) for s in range(count)])  24.3 us
    all_to_all x1, blocking collectives, per_device(): lax.all_to_all(jnp.broadcast_to(gap[None], (count, PAD, HD)), 'ctx', 0, 0)  18.3 us
    all_to_all x1, waiting for transfers between devices, per_device(): gathered = lax.all_to_all(spread, 'ctx', 0, 0, axis_index_groups=columns)  17 us
    ppermute x2, waiting for transfers between devices, raised(): lax.ppermute(value, 'ctx', [(s, (s + PLANE) % count) for s in range(count)])  13.4 us
    all_to_all x1, blocking collectives, per_device(): gap = jnp.sum(lax.all_to_all(gap, 'head', 0, 0), axis=0)  12.5 us
    all_to_all x1, starting transfers between devices, per_device(): gathered = lax.all_to_all(spread, 'ctx', 0, 0, axis_index_groups=columns)  8.99 us
    pallas_call x4, Pallas kernels, attend(): pl.pallas_call(functools.partial(attend_kernel, slots, first, last), out_...  8.97 us
  transfers between devices with their start and end apart: 21, of which 9 were waited for; matrix products, arithmetic and copies ran while one was open for 2% of the time, Pallas kernels for 6%

profile of v1, /device:TPU:1, one launch (start us, length us, event | category | flops | bytes accessed | tf_op | source)
XLA Modules:
  0.0 152.1 jit_solution(302000477431804774)
XLA Ops:
  0.6 3.3 %collective-permute-start.10 = (bf16[2,512,128]{2,1,0:T(8,128)(2,1)}, bf16[2,512,128]{2,1,0:T(8,128)(2,1)S(1)}, u32[]{:S(2)}, u32[]{:S(2)}) collective-permute-start(bf16[2,512,128]{2,1,0:T(8,128)(2,1)} %refs_3_.1), channel_id=1, source_target_pairs={{0,8},{8,0},{16,24},{24,16},{32,40},{40,32},{48,56},{56,48},{64,72... | collective-permute-start | bytes 786440 | tf_op jit(solution)/shard_map/ppermute | solution.py:268
  7.1 7.5 %collective-permute-done.refs_5_ = bf16[2,512,128]{2,1,0:T(8,128)(2,1)S(1)} collective-permute-done((bf16[2,512,128]{2,1,0:T(8,128)(2,1)}, bf16[2,512,128]{2,1,0:T(8,128)(2,1)S(1)}, u32[]{:S(2)}, u32[]{:S(2)}) %collective-permute-start) | collective-permute-done | bytes 262176 | tf_op jit(solution)/shard_map/ppermute | solution.py:273
  15.4 1.3 collective-permute-start.4
  17.1 5.9 %collective-permute-done.1.refs_5_ = bf16[2,512,128]{2,1,0:T(8,128)(2,1)S(1)} collective-permute-done((bf16[2,512,128]{2,1,0:T(8,128)(2,1)S(1)}, bf16[2,512,128]{2,1,0:T(8,128)(2,1)S(1)}, u32[]{:S(2)}, u32[]{:S(2)}) %collective-permute-start.1) | collective-permute-done | bytes 262176 | tf_op jit(solution)/shard_map/ppermute | solution.py:273
  23.0 1.3 collective-permute-start.2
  25.6 1.9 %collective-permute-start.6 = (bf16[2,512,128]{2,1,0:T(8,128)(2,1)S(1)}, bf16[2,512,128]{2,1,0:T(8,128)(2,1)S(1)}, u32[]{:S(2)}, u32[]{:S(2)}) collective-permute-start(bf16[2,512,128]{2,1,0:T(8,128)(2,1)S(1)} %collective-permute-done.1.refs_5_), channel_id=1, source_target_pairs={{0,8},{8,0},{16,24},{24,16},{32,40},{40,32},{48,56},{56,48},{64,72... | collective-permute-start | bytes 786440 | tf_op jit(solution)/shard_map/ppermute | solution.py:268
  27.6 4.2 %attend_2.2 = (f32[512,512]{1,0:T(8,128)S(1)}, f32[512,512]{1,0:T(8,128)S(1)}, f32[512,512]{1,0:T(8,128)S(1)}) custom-call(s32[1]{0:T(128)} %bitcast.refs_0_.me_ref, s32[7]{0:T(128)S(1)} %copy-done.1, bf16[512,512]{1,0:T(8,128)(2,1)S(1)} %copy-done, bf16[2,512,128]{2,1,0:T(8,128)(2,1)S(1)} %copy-done.4, bf16[2,512,128]{2,1,0:T(8,128)(2,1)S(1)} %collective-permute-done.10.refs_4_), custom_call_target="tpu_custom_call" | custom-call | flops 1073741824 | bytes 4194304 | tf_op jit(solution)/shard_map/attend_2/pallas_call | solution.py:184
  32.1 1.6 %attend_4.2 = (f32[512,512]{1,0:T(8,128)S(1)}, f32[512,512]{1,0:T(8,128)S(1)}, f32[512,512]{1,0:T(8,128)S(1)}) custom-call(s32[1]{0:T(128)} %bitcast.refs_0_.me_ref, s32[7]{0:T(128)S(1)} %copy-done.1, bf16[512,512]{1,0:T(8,128)(2,1)S(1)} %copy-done, ...), custom_call_target="tpu_custom_call", output_to_operand_aliasing={{0}: (7, {}), {1}: (8, {}), {2}: (9, {})} | custom-call | flops 2147483648 | bytes 4194304 | tf_op jit(solution)/shard_map/attend_4/pallas_call | solution.py:184
  33.7 5.3 %collective-permute-start.14 = (bf16[1792,256]{1,0:T(8,128)(2,1)S(1)}, bf16[1792,256]{1,0:T(8,128)(2,1)S(1)}, u32[]{:S(2)}, u32[]{:S(2)}) collective-permute-start(bf16[1792,256]{1,0:T(8,128)(2,1)S(1)} %constant_dynamic-update-slice_fusion.refs_0_), channel_id=1, source_target_pairs={{0,16},{8,24},{16,0},{24,8},{32,48},{40,56},{48,32},{56,40},{64,80... | collective-permute-start | bytes 2752520 | tf_op jit(solution)/shard_map/ppermute | solution.py:268
  40.2 2.0 %attend_2.3 = (f32[512,512]{1,0:T(8,128)}, bf16[64,512]{1,0:T(8,128)(2,1)S(1)}, bf16[64,512]{1,0:T(8,128)(2,1)S(1)}, bf16[128,512]{1,0:T(8,128)(2,1)S(1)}) custom-call(s32[1]{0:T(128)} %bitcast.refs_0_.me_ref, s32[7]{0:T(128)S(1)} %copy-done.1, bf16[512,512]{1,0:T(8,128)(2,1)S(1)} %copy-done, bf16[2,512,128]{2,1,0:T(8,128)(2,1)S(1)} %collective-permute-done.2.refs_3_, ...), custom_call_target="tpu_custom_call" | custom-call | flops 1073741824 | bytes 4194304 | tf_op jit(solution)/shard_map/attend_2/pallas_call | solution.py:184
  44.2 17.0 %collective-permute-done.12 = bf16[64,512]{1,0:T(8,128)(2,1)S(1)} collective-permute-done((bf16[64,512]{1,0:T(8,128)(2,1)S(1)}, bf16[64,512]{1,0:T(8,128)(2,1)S(1)}, u32[]{:S(2)}, u32[]{:S(2)}) %collective-permute-start.12) | collective-permute-done | bytes 65568 | tf_op jit(solution)/shard_map/ppermute | solution.py:268
  62.0 9.0 %all-to-all-start = ((bf16[8,64,512]{2,1,0:T(8,128)(2,1)}), bf16[8,64,512]{2,1,0:T(8,128)(2,1)S(1)}, u32[]{:S(2)}, u32[]{:S(2)}) async-start(bf16[8,64,512]{2,1,0:T(8,128)(2,1)} %broadcast_in_dim.4), calls=%async_computation | async-start | bytes 1048576 | tf_op jit(solution)/shard_map/all_to_all | solution.py:351
  72.0 17.0 %all-to-all-done.got_ref = bf16[8,64,512]{2,1,0:T(8,128)(2,1)S(1)} async-done(((bf16[8,64,512]{2,1,0:T(8,128)(2,1)}), bf16[8,64,512]{2,1,0:T(8,128)(2,1)S(1)}, u32[]{:S(2)}, u32[]{:S(2)}) %all-to-all-start) | async-done | bytes 524320 | tf_op jit(solution)/shard_map/all_to_all | solution.py:351
  89.0 1.5 project.1
  91.7 3.4 %collective-permute-done.16 = bf16[64,1024]{1,0:T(8,128)(2,1)S(1)} collective-permute-done((bf16[64,1024]{1,0:T(8,128)(2,1)S(1)}, bf16[64,1024]{1,0:T(8,128)(2,1)S(1)}, u32[]{:S(2)}, u32[]{:S(2)}) %collective-permute-start.16) | collective-permute-done | bytes 131104 | tf_op jit(solution)/shard_map/ppermute | solution.py:268
  95.1 2.8 %collective-permute-start.17 = (bf16[64,1024]{1,0:T(8,128)(2,1)S(1)}, bf16[64,1024]{1,0:T(8,128)(2,1)S(1)}, u32[]{:S(2)}, u32[]{:S(2)}) collective-permute-start(bf16[64,1024]{1,0:T(8,128)(2,1)S(1)} %add.32), channel_id=1, source_target_pairs={{0,4},{1,5},{2,6},{3,7},{4,0},{5,1},{6,2},{7,3},{8,12},{9,13},{10,... | collective-permute-start | bytes 393224 | tf_op jit(solution)/shard_map/ppermute | solution.py:268
  97.9 2.6 %collective-permute-done.17 = bf16[64,1024]{1,0:T(8,128)(2,1)S(1)} collective-permute-done((bf16[64,1024]{1,0:T(8,128)(2,1)S(1)}, bf16[64,1024]{1,0:T(8,128)(2,1)S(1)}, u32[]{:S(2)}, u32[]{:S(2)}) %collective-permute-start.17) | collective-permute-done | bytes 131104 | tf_op jit(solution)/shard_map/ppermute | solution.py:268
  100.6 2.5 %collective-permute-start.18 = (bf16[64,1024]{1,0:T(8,128)(2,1)S(1)}, bf16[64,1024]{1,0:T(8,128)(2,1)S(1)}, u32[]{:S(2)}, u32[]{:S(2)}) collective-permute-start(bf16[64,1024]{1,0:T(8,128)(2,1)S(1)} %add.33.mine_ref), channel_id=1, source_target_pairs={{0,1},{1,0},{2,3},{3,2},{4,5},{5,4},{6,7},{7,6},{8,9},{9,8},{10,11... | collective-permute-start | bytes 393224 | tf_op jit(solution)/shard_map/ppermute | solution.py:268
  103.1 2.9 %collective-permute-done.18.other_ref = bf16[64,1024]{1,0:T(8,128)(2,1)S(1)} collective-permute-done((bf16[64,1024]{1,0:T(8,128)(2,1)S(1)}, bf16[64,1024]{1,0:T(8,128)(2,1)S(1)}, u32[]{:S(2)}, u32[]{:S(2)}) %collective-permute-start.18) | collective-permute-done | bytes 131104 | tf_op jit(solution)/shard_map/ppermute | solution.py:268
  106.0 2.3 %inner.1 = bf16[64,1024]{1,0:T(8,128)(2,1)} custom-call(s32[1]{0:T(128)} %bitcast.refs_0_.me_ref, bf16[64,1024]{1,0:T(8,128)(2,1)S(1)} %add.33.mine_ref, bf16[64,1024]{1,0:T(8,128)(2,1)S(1)} %collective-permute-done.18.other_ref, bf16[1792,256]{1,0:T(8,128)(2,1)S(1)} %constant_dynamic-update-slice_fusion.refs_0_, ...), custom_call_target="tpu_custom_call" | custom-call | tf_op jit(solution)/shard_map/inner/pallas_call | solution.py:200
  108.3 3.5 %all-to-all-start.1 = ((bf16[8,8,1024]{2,1,0:T(8,128)(2,1)}), bf16[8,8,1024]{2,1,0:T(8,128)(2,1)S(1)}, u32[]{:S(2)}, u32[]{:S(2)}) async-start(bf16[8,8,1024]{2,1,0:T(8,128)(2,1)} %bitcast.5), calls=%async_computation.1 | async-start | bytes 262144 | tf_op jit(solution)/shard_map/all_to_all | solution.py:367
  112.0 7.6 %all-to-all-done.1.got_ref = bf16[8,8,1024]{2,1,0:T(8,128)(2,1)S(1)} async-done(((bf16[8,8,1024]{2,1,0:T(8,128)(2,1)}), bf16[8,8,1024]{2,1,0:T(8,128)(2,1)S(1)}, u32[]{:S(2)}, u32[]{:S(2)}) %all-to-all-start.1) | async-done | bytes 131104 | tf_op jit(solution)/shard_map/all_to_all | solution.py:367
  119.9 12.5 %all_to_all.20 = f32[8,8,128]{2,1,0:T(8,128)S(1)} all-to-all(f32[8,8,128]{2,1,0:T(8,128)S(1)} %hidden.1), channel_id=1, replica_groups=mesh['ctx'=32,'head'=8] {'head'}, dimensions={0} | all-to-all | bytes 65536 | tf_op jit(solution)/shard_map/all_to_all | solution.py:378
  132.5 18.3 %all_to_all.21.got_ref = f32[32,8,128]{2,1,0:T(8,128)S(1)} all-to-all(f32[32,8,128]{2,1,0:T(8,128)S(1)} %broadcast_in_dim.5), channel_id=1, replica_groups=mesh['ctx'=32,'head'=8] {'ctx'}, dimensions={0} | all-to-all | bytes 262144 | tf_op jit(solution)/shard_map/all_to_all | solution.py:379
  (68 shorter events, 13.9 us)
Async XLA Ops:
  0.6 5.5 %copy-start.5 = (bf16[256,1024]{1,0:T(8,128)(2,1)S(1)}, bf16[256,1024]{1,0:T(8,128)(2,1)}, u32[]{:S(2)}) copy-start(bf16[256,1024]{1,0:T(8,128)(2,1)} %param.18) | copy-start | bytes 1572868
  0.6 24.9 %collective-permute-start.10 = (bf16[2,512,128]{2,1,0:T(8,128)(2,1)}, bf16[2,512,128]{2,1,0:T(8,128)(2,1)S(1)}, u32[]{:S(2)}, u32[]{:S(2)}) collective-permute-start(bf16[2,512,128]{2,1,0:T(8,128)(2,1)} %refs_3_.1), channel_id=1, source_target_pairs={{0,8},{8,0},{16,24},{24,16},{32,40},{40,32},{48,56},{56,48},{64,72... | collective-permute-start | bytes 786440 | tf_op jit(solution)/shard_map/ppermute | solution.py:268
  4.0 10.6 %collective-permute-start = (bf16[2,512,128]{2,1,0:T(8,128)(2,1)}, bf16[2,512,128]{2,1,0:T(8,128)(2,1)S(1)}, u32[]{:S(2)}, u32[]{:S(2)}) collective-permute-start(bf16[2,512,128]{2,1,0:T(8,128)(2,1)} %refs_3_.1), channel_id=1, source_target_pairs={{0,32},{8,40},{16,48},{24,56},{32,64},{40,72},{48,80},{56,88},{64,... | collective-permute-start | bytes 786440 | tf_op jit(solution)/shard_map/ppermute | solution.py:273
  4.0 12.8 %collective-permute-start.7 = (bf16[2,512,128]{2,1,0:T(8,128)(2,1)}, bf16[2,512,128]{2,1,0:T(8,128)(2,1)S(1)}, u32[]{:S(2)}, u32[]{:S(2)}) collective-permute-start(bf16[2,512,128]{2,1,0:T(8,128)(2,1)} %refs_3_.1), channel_id=1, source_target_pairs={{0,16},{8,24},{16,0},{24,8},{32,48},{40,56},{48,32},{56,40},{64,80... | collective-permute-start | bytes 786440 | tf_op jit(solution)/shard_map/ppermute | solution.py:268
  14.6 8.4 %collective-permute-start.1 = (bf16[2,512,128]{2,1,0:T(8,128)(2,1)S(1)}, bf16[2,512,128]{2,1,0:T(8,128)(2,1)S(1)}, u32[]{:S(2)}, u32[]{:S(2)}) collective-permute-start(bf16[2,512,128]{2,1,0:T(8,128)(2,1)S(1)} %collective-permute-done.refs_5_), channel_id=1, source_target_pairs={{0,32},{8,40},{16,48},{24,56},{32,64},{40,72},{48,80},{56,88},{64,... | collective-permute-start | bytes 786440 | tf_op jit(solution)/shard_map/ppermute | solution.py:273
  14.7 17.4 %collective-permute-start.9 = (bf16[2,512,128]{2,1,0:T(8,128)(2,1)S(1)}, bf16[2,512,128]{2,1,0:T(8,128)(2,1)S(1)}, u32[]{:S(2)}, u32[]{:S(2)}) collective-permute-start(bf16[2,512,128]{2,1,0:T(8,128)(2,1)S(1)} %collective-permute-done.refs_5_), channel_id=1, source_target_pairs={{0,8},{8,0},{16,24},{24,16},{32,40},{40,32},{48,56},{56,48},{64,72... | collective-permute-start | bytes 786440 | tf_op jit(solution)/shard_map/ppermute | solution.py:268
  15.4 12.0 %collective-permute-start.4 = (bf16[2,512,128]{2,1,0:T(8,128)(2,1)S(1)}, bf16[2,512,128]{2,1,0:T(8,128)(2,1)S(1)}, u32[]{:S(2)}, u32[]{:S(2)}) collective-permute-start(bf16[2,512,128]{2,1,0:T(8,128)(2,1)S(1)} %collective-permute-done.refs_5_), channel_id=1, source_target_pairs={{0,16},{8,24},{16,0},{24,8},{32,48},{40,56},{48,32},{56,40},{64,80... | collective-permute-start | bytes 786440 | tf_op jit(solution)/shard_map/ppermute | solution.py:268
  16.8 15.3 %collective-permute-start.8 = (bf16[2,512,128]{2,1,0:T(8,128)(2,1)S(1)}, bf16[2,512,128]{2,1,0:T(8,128)(2,1)}, u32[]{:S(2)}, u32[]{:S(2)}) collective-permute-start(bf16[2,512,128]{2,1,0:T(8,128)(2,1)S(1)} %collective-permute-done.7.refs_3_), channel_id=1, source_target_pairs={{0,8},{8,0},{16,24},{24,16},{32,40},{40,32},{48,56},{56,48},{64,72... | collective-permute-start | bytes 786440 | tf_op jit(solution)/shard_map/ppermute | solution.py:268
  23.0 8.8 %collective-permute-start.2 = (bf16[2,512,128]{2,1,0:T(8,128)(2,1)S(1)}, bf16[2,512,128]{2,1,0:T(8,128)(2,1)S(1)}, u32[]{:S(2)}, u32[]{:S(2)}) collective-permute-start(bf16[2,512,128]{2,1,0:T(8,128)(2,1)S(1)} %collective-permute-done.1.refs_5_), channel_id=1, source_target_pairs={{0,16},{8,24},{16,0},{24,8},{32,48},{40,56},{48,32},{56,40},{64,80... | collective-permute-start | bytes 786440 | tf_op jit(solution)/shard_map/ppermute | solution.py:268
  25.6 13.5 %collective-permute-start.6 = (bf16[2,512,128]{2,1,0:T(8,128)(2,1)S(1)}, bf16[2,512,128]{2,1,0:T(8,128)(2,1)S(1)}, u32[]{:S(2)}, u32[]{:S(2)}) collective-permute-start(bf16[2,512,128]{2,1,0:T(8,128)(2,1)S(1)} %collective-permute-done.1.refs_5_), channel_id=1, source_target_pairs={{0,8},{8,0},{16,24},{24,16},{32,40},{40,32},{48,56},{56,48},{64,72... | collective-permute-start | bytes 786440 | tf_op jit(solution)/shard_map/ppermute | solution.py:268
  27.5 11.5 %collective-permute-start.5 = (bf16[2,512,128]{2,1,0:T(8,128)(2,1)S(1)}, bf16[2,512,128]{2,1,0:T(8,128)(2,1)S(1)}, u32[]{:S(2)}, u32[]{:S(2)}) collective-permute-start(bf16[2,512,128]{2,1,0:T(8,128)(2,1)S(1)} %collective-permute-done.4.refs_3_), channel_id=1, source_target_pairs={{0,8},{8,0},{16,24},{24,16},{32,40},{40,32},{48,56},{56,48},{64,72... | collective-permute-start | bytes 786440 | tf_op jit(solution)/shard_map/ppermute | solution.py:268
  31.8 8.4 %collective-permute-start.3 = (bf16[2,512,128]{2,1,0:T(8,128)(2,1)S(1)}, bf16[2,512,128]{2,1,0:T(8,128)(2,1)S(1)}, u32[]{:S(2)}, u32[]{:S(2)}) collective-permute-start(bf16[2,512,128]{2,1,0:T(8,128)(2,1)S(1)} %collective-permute-done.2.refs_3_), channel_id=1, source_target_pairs={{0,8},{8,0},{16,24},{24,16},{32,40},{40,32},{48,56},{56,48},{64,72... | collective-permute-start | bytes 786440 | tf_op jit(solution)/shard_map/ppermute | solution.py:268
  33.7 37.3 %collective-permute-start.14 = (bf16[1792,256]{1,0:T(8,128)(2,1)S(1)}, bf16[1792,256]{1,0:T(8,128)(2,1)S(1)}, u32[]{:S(2)}, u32[]{:S(2)}) collective-permute-start(bf16[1792,256]{1,0:T(8,128)(2,1)S(1)} %constant_dynamic-update-slice_fusion.refs_0_), channel_id=1, source_target_pairs={{0,16},{8,24},{16,0},{24,8},{32,48},{40,56},{48,32},{56,40},{64,80... | collective-permute-start | bytes 2752520 | tf_op jit(solution)/shard_map/ppermute | solution.py:268
  42.2 1.3 collective-permute-start.11
  43.6 17.5 %collective-permute-start.12 = (bf16[64,512]{1,0:T(8,128)(2,1)S(1)}, bf16[64,512]{1,0:T(8,128)(2,1)S(1)}, u32[]{:S(2)}, u32[]{:S(2)}) collective-permute-start(bf16[64,512]{1,0:T(8,128)(2,1)S(1)} %slice_add_fusion), channel_id=1, source_target_pairs={{0,16},{8,24},{16,0},{24,8},{32,48},{40,56},{48,32},{56,40},{64,80... | collective-permute-start | bytes 196616 | tf_op jit(solution)/shard_map/ppermute | solution.py:268
  43.7 28.2 %collective-permute-start.13 = (bf16[1792,256]{1,0:T(8,128)(2,1)S(1)}, bf16[1792,256]{1,0:T(8,128)(2,1)S(1)}, u32[]{:S(2)}, u32[]{:S(2)}) collective-permute-start(bf16[1792,256]{1,0:T(8,128)(2,1)S(1)} %constant_dynamic-update-slice_fusion.refs_0_), channel_id=1, source_target_pairs={{0,8},{8,0},{16,24},{24,16},{32,40},{40,32},{48,56},{56,48},{64,72... | collective-permute-start | bytes 2752520 | tf_op jit(solution)/shard_map/ppermute | solution.py:268
  62.0 26.9 %all-to-all-start = ((bf16[8,64,512]{2,1,0:T(8,128)(2,1)}), bf16[8,64,512]{2,1,0:T(8,128)(2,1)S(1)}, u32[]{:S(2)}, u32[]{:S(2)}) async-start(bf16[8,64,512]{2,1,0:T(8,128)(2,1)} %broadcast_in_dim.4), calls=%async_computation | async-start | bytes 1048576 | tf_op jit(solution)/shard_map/all_to_all | solution.py:351
  71.0 18.0 %collective-permute-start.15 = (bf16[1792,256]{1,0:T(8,128)(2,1)S(1)}, bf16[1792,256]{1,0:T(8,128)(2,1)}, u32[]{:S(2)}, u32[]{:S(2)}) collective-permute-start(bf16[1792,256]{1,0:T(8,128)(2,1)S(1)} %collective-permute-done.14.refs_2_), channel_id=1, source_target_pairs={{0,8},{8,0},{16,24},{24,16},{32,40},{40,32},{48,56},{56,48},{64,72... | collective-permute-start | bytes 2752520 | tf_op jit(solution)/shard_map/ppermute | solution.py:268
  90.4 4.7 %collective-permute-start.16 = (bf16[64,1024]{1,0:T(8,128)(2,1)S(1)}, bf16[64,1024]{1,0:T(8,128)(2,1)S(1)}, u32[]{:S(2)}, u32[]{:S(2)}) collective-permute-start(bf16[64,1024]{1,0:T(8,128)(2,1)S(1)} %project.1), channel_id=1, source_target_pairs={{0,2},{1,3},{2,0},{3,1},{4,6},{5,7},{6,4},{7,5},{8,10},{9,11},{10,... | collective-permute-start | bytes 393224 | tf_op jit(solution)/shard_map/ppermute | solution.py:268
  95.1 5.4 %collective-permute-start.17 = (bf16[64,1024]{1,0:T(8,128)(2,1)S(1)}, bf16[64,1024]{1,0:T(8,128)(2,1)S(1)}, u32[]{:S(2)}, u32[]{:S(2)}) collective-permute-start(bf16[64,1024]{1,0:T(8,128)(2,1)S(1)} %add.32), channel_id=1, source_target_pairs={{0,4},{1,5},{2,6},{3,7},{4,0},{5,1},{6,2},{7,3},{8,12},{9,13},{10,... | collective-permute-start | bytes 393224 | tf_op jit(solution)/shard_map/ppermute | solution.py:268
  100.6 5.4 %collective-permute-start.18 = (bf16[64,1024]{1,0:T(8,128)(2,1)S(1)}, bf16[64,1024]{1,0:T(8,128)(2,1)S(1)}, u32[]{:S(2)}, u32[]{:S(2)}) collective-permute-start(bf16[64,1024]{1,0:T(8,128)(2,1)S(1)} %add.33.mine_ref), channel_id=1, source_target_pairs={{0,1},{1,0},{2,3},{3,2},{4,5},{5,4},{6,7},{7,6},{8,9},{9,8},{10,11... | collective-permute-start | bytes 393224 | tf_op jit(solution)/shard_map/ppermute | solution.py:268
  108.3 11.3 %all-to-all-start.1 = ((bf16[8,8,1024]{2,1,0:T(8,128)(2,1)}), bf16[8,8,1024]{2,1,0:T(8,128)(2,1)S(1)}, u32[]{:S(2)}, u32[]{:S(2)}) async-start(bf16[8,8,1024]{2,1,0:T(8,128)(2,1)} %bitcast.5), calls=%async_computation.1 | async-start | bytes 262144 | tf_op jit(solution)/shard_map/all_to_all | solution.py:367
  132.4 18.4 %copy-start.2 = (s32[7]{0:T(128)S(1)}, s32[7]{0:T(128)}, u32[]{:S(2)}) copy-start(s32[7]{0:T(128)} %prompts.1) | copy-start | bytes 88
  132.5 18.4 %copy-start.3 = (s32[7]{0:T(128)S(1)}, s32[7]{0:T(128)}, u32[]{:S(2)}) copy-start(s32[7]{0:T(128)} %clusters.1) | copy-start | bytes 88
  (5 other events, 11.6 us)
